TPU v7x, 256 devices: a whole 4x4x8 slice. The times are simulated.
256 devices in a mesh: dp: 8 (over x, core), bal: 32 (over y, z).
Axes of the slice: x: 4, y: 4, z: 8, core: 2. Of those that a mesh axis runs over, the one named last changes fastest.
Arguments:
- patches: bfloat16 [512, 256, 1152], P(('dp', 'bal')), parts along dimension 0, may hold values from -6 to 6
- counts: int32 [128], P('dp'), parts along dimension 0, may hold values from 1 to 8, 64 in all
- owner_pick: int32 [128], P('dp'), parts along dimension 0, may hold values from 0 to 59
- ln_gain: float32 [1152], replicated, may hold values from 0.1 to 1.9
- ln_bias: float32 [1152], replicated, may hold values from -3 to 3
- w_qkv: bfloat16 [1152, 1728], replicated, may hold values from -0.1875 to 0.1875
- w_out: bfloat16 [576, 1152], replicated, may hold values from -0.25 to 0.25
- ctx_gain: float32 [1152], replicated, may hold values from 0.1 to 1.9
- w_kv: bfloat16 [1152, 768], replicated, may hold values from -0.1875 to 0.1875
- latent_queries: bfloat16 [64, 1536], replicated, may hold values from -160 to 160
- latent_kv: bfloat16 [64, 768], replicated, may hold values from -6 to 6
Outputs:
- resampled: bfloat16 [256, 2, 64, 1536], P(('dp', 'bal')), parts along dimension 0
There are 8 independent parts, one for each index of `dp`. A program takes and returns all parts, laid end to end along the dimension named above; an argument that names none is the same for every part. Nothing has to cross between parts.
Inputs may be any that keep to these rules, and one draw needn't show every extreme that they name: `owner_pick`: the choice of each image's owner among the devices holding its tiles.
All inputs are finite; a program needn't handle non-finite values.
Results may differ from a plain program's by a relative error of at most 0.02.
Values may be sent and summed in bfloat16 or wider, within the bound.
A program may use at most 128 MiB of HBM per device.

v0:
```python
import functools
import math

import jax
import jax.numpy as jnp
from jax import lax
from jax.experimental import pallas as pl
from jax.experimental.pallas import tpu as pltpu
from jax.sharding import PartitionSpec as P

D = 1152
HA = 8
HS = 72
PATCHES = 256
QH = 16
KVH = 4
RD = 96
LAT = 64
T = 2
IMAGES = 16
REACH = 4
ROWS = T * PATCHES
KW = KVH * RD
EPS = 1e-6
NEG = -1e30
LOG2E = math.log2(math.e)
C_TOWER = LOG2E / math.sqrt(HS)
C_RES = LOG2E / math.sqrt(RD)
MESH = pl.DeviceIdType.MESH
F32 = jnp.float32
BF = jnp.bfloat16
NT = (((1,), (1,)), ((), ()))
KWIN = ((0, 128), (0, 256), (128, 256), (256, 128))


def lanes(shape):
    return lax.broadcasted_iota(jnp.int32, shape, len(shape) - 1)


def dot(a, b):
    return jnp.dot(a, b, preferred_element_type=F32)


def dot_nt(a, b):
    return lax.dot_general(a, b, NT, preferred_element_type=F32)


def roll(x, shift):
    shift = shift % x.shape[-1]
    return x if shift == 0 else pltpu.roll(x, shift, 1)


def kernel(
    patches,
    counts,
    picks,
    ln_gain,
    ln_bias,
    w_qkv,
    w_out,
    ctx_gain,
    w_kv,
    latent_q,
    latent_kv,
    out,
    xb,
    wq,
    wo,
    wk,
    nb,
    pk,
    qr,
    mix,
    fg,
    cx,
    vk,
    qx,
    lq,
    lkv,
    send_o,
    send_s,
    got_o,
    got_s,
    lat_o,
    lat_s,
    load_sem,
    send_sem,
    recv_sem,
):
    me = lax.axis_index("bal")
    dp = lax.axis_index("dp")
    n = lax.axis_size("bal")
    right = lax.rem(me + 1, n)
    left = lax.rem(me + n - 1, n)
    sides = ((dp, right), (dp, left))

    loads = []

    def load(src, dst):
        copy = pltpu.make_async_copy(src, dst, load_sem.at[len(loads)])
        copy.start()
        loads.append(copy)
        return copy

    x_loads = [load(patches.at[t], xb.at[pl.ds(t * PATCHES, PATCHES)]) for t in range(T)]
    cuts = [(j * 256, min(256, 3 * HA * HS - j * 256)) for j in range(7)]
    q_loads = [load(w_qkv.at[pl.ds(a, w)], wq.at[pl.ds(a, w)]) for a, w in cuts]
    lq_load = load(latent_q, lq)
    lkv_load = load(latent_kv, lkv)
    wo_load = load(w_out, wo)
    wk_load = load(w_kv, wk)

    barrier = pltpu.get_barrier_semaphore()
    for side in sides:
        pl.semaphore_signal(barrier, inc=1, device_id=side, device_id_type=MESH)

    gain = ln_gain[...].reshape(1, D)
    bias = ln_bias[...].reshape(1, D)

    RB = 16
    for t in range(T):
        x_loads[t].wait()

        def norm(i, _, t=t):
            rows = pl.ds(pl.multiple_of(t * PATCHES + i * RB, RB), RB)
            x = xb[rows, :].astype(F32)
            mean = jnp.mean(x, axis=-1, keepdims=True)
            c = x - mean
            var = jnp.mean(c * c, axis=-1, keepdims=True)
            nb[rows, :] = (c * lax.rsqrt(var + EPS) * gain + bias).astype(BF)
            return 0

        lax.fori_loop(0, PATCHES // RB, norm, 0, unroll=2)

    for j, (a, w) in enumerate(cuts):
        q_loads[j].wait()
        res = dot_nt(nb[...], wq[pl.ds(a, w), :]).astype(BF)
        if w < 256:
            res = jnp.concatenate([res, jnp.zeros((ROWS, 256 - w), BF)], axis=1)
        pk[:, pl.ds(a, 256)] = res

    def shift_q(i, _):
        rows = pl.ds(pl.multiple_of(i * 32, 32), 32)
        ln = lanes((32, 128))
        before = jnp.zeros((32, 128), F32)
        for j in range(5):
            now = roll(pk[rows, pl.ds(j * 128, 128)].astype(F32), 64)
            qr[rows, pl.ds(j * 128, 128)] = jnp.where(ln < 64, before, now).astype(BF)
            before = now
        return 0

    lax.fori_loop(0, ROWS // 32, shift_q, 0)

    def tower(t, _):
        rows = pl.ds(pl.multiple_of(t * PATCHES, PATCHES), PATCHES)
        ln = lanes((PATCHES, 256))
        before = jnp.zeros((PATCHES, 128), F32)
        for i in range(HA // 2):
            q = qr[rows, pl.ds(128 * i, 256)]
            k = pk[rows, pl.ds(512 + 128 * i, 256)]
            v = pk[rows, pl.ds(1152 + 128 * i, 256)]
            mixed = jnp.zeros((PATCHES, 256), F32)
            for h in range(2):
                lo = 64 + 16 * i + HS * h
                mine = jnp.logical_and(ln >= lo, ln < lo + HS)
                s = dot_nt(jnp.where(mine, q, jnp.zeros_like(q)), k)
                top = jnp.max(s, axis=-1, keepdims=True)
                e = jnp.exp2((s - top) * C_TOWER)
                total = jnp.sum(e, axis=-1, keepdims=True)
                o = dot(e.astype(BF), v) * (1.0 / total)
                lo = 16 * i + HS * h
                mixed = jnp.where(jnp.logical_and(ln >= lo, ln < lo + HS), o, mixed)
            mix[rows, pl.ds(128 * i, 128)] = (before + mixed[:, :128]).astype(BF)
            before = mixed[:, 128:]
        mix[rows, pl.ds(512, 128)] = before.astype(BF)
        return 0

    lax.fori_loop(0, T, tower, 0)

    wo_load.wait()
    gain_c = ctx_gain[...].reshape(1, D)
    square = jnp.zeros((ROWS, 128), F32)
    for a in range(0, D, 256):
        w = min(256, D - a)
        f = dot(mix[:, : HA * HS], wo[:, pl.ds(a, w)]) + xb[:, pl.ds(a, w)].astype(F32)
        f = f.astype(BF).astype(F32)
        for b in range(0, w, 128):
            square = square + f[:, b : b + 128] * f[:, b : b + 128]
        fg[:, pl.ds(a, w)] = (f * gain_c[:, a : a + w]).astype(BF)
    factor = lax.rsqrt(jnp.sum(square, axis=-1, keepdims=True) * (1.0 / D) + EPS)

    wk_load.wait()
    for a in range(0, 2 * KW, 256):
        cx[:, pl.ds(a, 256)] = (dot(fg[...], wk[:, pl.ds(a, 256)]) * factor).astype(BF)

    lq_load.wait()
    lkv_load.wait()
    ln = lanes((LAT, 128))
    for k in range(KVH):
        qt = [lq[:, pl.ds(k * KW + 128 * j, 128)].astype(F32) for j in range(3)]
        first, width = KWIN[k]
        for g in range(4):
            parts = []
            for b in range(first, first + width, 128):
                move = b - RD * k + RD * g
                acc = jnp.zeros((LAT, 128), F32)
                for j in range(3):
                    lo = max(RD * k, b, 128 * j - move + b) - b
                    hi = min(RD * k + RD, b + 128, 128 * j + 128 - move + b) - b
                    if hi > lo:
                        moved = roll(qt[j], 128 * j - move)
                        acc = jnp.where(jnp.logical_and(ln >= lo, ln < hi), moved, acc)
                parts.append(acc)
            qx[k, pl.ds(g * LAT, LAT), pl.ds(0, width)] = jnp.concatenate(parts, axis=1).astype(BF)

    def head_values(ref, rows, count, k):
        ln = lanes((count, 128))
        lo = RD * k
        a = lo // 128
        shift = -(lo - 128 * a)
        one = roll(ref[rows, pl.ds(KW + 128 * a, 128)].astype(F32), shift)
        if lo + RD > 128 * (a + 1):
            two = roll(ref[rows, pl.ds(KW + 128 * (a + 1), 128)].astype(F32), shift)
            one = jnp.where(ln < 128 + shift, one, two)
        return one.astype(BF)

    def head_state(ref, rows, count, k):
        first, width = KWIN[k]
        s = dot_nt(qx[k, :, pl.ds(0, width)], ref[rows, pl.ds(first, width)])
        top = jnp.max(s, axis=-1, keepdims=True)
        e = jnp.exp2((s - top) * C_RES)
        total = jnp.sum(e, axis=-1, keepdims=True)
        o = dot(e.astype(BF), head_values(ref, rows, count, k)) * (1.0 / total)
        return top * C_RES + jnp.log2(total), o

    def dense(o):
        p = [roll(o[LAT * g : LAT * g + LAT], RD * g) for g in range(4)]
        return jnp.concatenate(
            [
                jnp.where(ln < 96, p[0], p[1]),
                jnp.where(ln < 64, p[1], p[2]),
                jnp.where(ln < 32, p[2], p[3]),
            ],
            axis=1,
        )

    def compact(table, lse, k):
        for g in range(4):
            column = jnp.broadcast_to(lse[LAT * g : LAT * g + LAT], (LAT, 128))
            table = jnp.where(ln == 4 * k + g, column, table)
        return table

    ends = []
    run = jnp.int32(0)
    for i in range(IMAGES):
        run = run + counts[i]
        ends.append(run)

    def image_of(tile):
        found = jnp.int32(0)
        for i in range(IMAGES):
            found = found + jnp.where(ends[i] <= tile, 1, 0)
        return found

    firsts = {d: image_of(2 * (me + d)) for d in range(0, REACH + 1)}
    lasts = {d: jnp.where(me + d < 0, -1, image_of(2 * (me + d) + 1)) for d in range(-REACH, 1)}
    img0, img1 = firsts[0], lasts[0]
    same = img0 == img1

    def owner_of(image):
        begin, end, pick = jnp.int32(0), jnp.int32(0), jnp.int32(0)
        for i in range(IMAGES):
            hit = image == i
            begin = jnp.where(hit, ends[i] - counts[i], begin)
            end = jnp.where(hit, ends[i], end)
            pick = jnp.where(hit, picks[i], pick)
        first, last = begin // 2, (end - 1) // 2
        return first + lax.rem(pick, last - first + 1)

    def flag(cond):
        return jnp.where(cond, F32(1.0), F32(0.0))

    def block(cond):
        return jnp.where(cond, F32(0.0), F32(NEG))

    has0 = flag(owner_of(img0) == me)
    has1 = flag(jnp.logical_and(owner_of(img1) == me, jnp.logical_not(same)))
    both = block(same)

    def copies(side, r, c):
        if c < KVH:
            src = send_o.at[side, c] if r == 0 else got_o.at[side, r - 1, c]
            dst = got_o.at[side, r, c]
        else:
            src = send_s.at[side] if r == 0 else got_s.at[side, r - 1]
            dst = got_s.at[side, r]
        return pltpu.make_async_remote_copy(
            src_ref=src,
            dst_ref=dst,
            send_sem=send_sem.at[side, r, c],
            recv_sem=recv_sem.at[side, r, c],
            device_id=sides[side],
            device_id_type=MESH,
        )

    tables = [jnp.zeros((LAT, 128), F32) for _ in range(3)]
    pl.semaphore_wait(barrier, 2)
    for k in range(KVH):
        l0, o0 = head_state(cx, pl.ds(0, PATCHES), PATCHES, k)
        l1, o1 = head_state(cx, pl.ds(PATCHES, PATCHES), PATCHES, k)
        pairs = ((l1, l0 + both), (l1 + both, l0))
        for side, (a, b) in enumerate(pairs):
            top = jnp.maximum(a, b)
            ea, eb = jnp.exp2(a - top), jnp.exp2(b - top)
            total = ea + eb
            inv = 1.0 / total
            tables[side] = compact(tables[side], top + jnp.log2(total), k)
            send_o[side, k] = dense(o1 * (ea * inv) + o0 * (eb * inv)).astype(BF)
            copies(side, 0, k).start()
        ll, ol = head_state(lkv, pl.ds(0, LAT), LAT, k)
        tables[2] = compact(tables[2], ll, k)
        lat_o[k] = dense(ol)
    for side in range(2):
        send_s[side] = tables[side]
        copies(side, 0, KVH).start()
    lat_s[...] = tables[2]

    order = (KVH,) + tuple(range(KVH))
    for r in range(REACH):
        for c in order:
            for side in range(2):
                copies(side, r, c).wait_recv()
                if r + 1 < REACH:
                    copies(side, r + 1, c).start()

    lr = [got_s[0, r] + block(lasts[-1 - r] == img0) for r in range(REACH)]
    ll0 = [got_s[1, r] + block(firsts[1 + r] == img0) for r in range(REACH)]
    ll1 = [got_s[1, r] + block(firsts[1 + r] == img1) for r in range(REACH)]
    slots = (
        [tables[1], tables[2]] + lr + ll0,
        [tables[0], tables[2]] + ll1,
    )
    weights = []
    for slot, has in zip(slots, (has0, has1)):
        top = functools.reduce(jnp.maximum, slot)
        es = [jnp.exp2(v - top) for v in slot]
        inv = has / functools.reduce(jnp.add, es)
        weights.append([e * inv for e in es])

    def spread(w, k):
        p = [jnp.broadcast_to(w[:, 4 * k + g : 4 * k + g + 1], (LAT, 128)) for g in range(4)]
        return jnp.concatenate(
            [jnp.where(ln < 96, p[0], p[1]), jnp.where(ln < 64, p[1], p[2]), jnp.where(ln < 32, p[2], p[3])],
            axis=1,
        )

    for k in range(KVH):
        sources = (
            [send_o[1, k], lat_o[k]]
            + [got_o[0, r, k] for r in range(REACH)]
            + [got_o[1, r, k] for r in range(REACH)],
            [send_o[0, k], lat_o[k]] + [got_o[1, r, k] for r in range(REACH)],
        )
        for slot in range(2):
            total = jnp.zeros((LAT, KW), F32)
            for w, o in zip(weights[slot], sources[slot]):
                total = total + spread(w, k) * o.astype(F32)
            out[0, slot, :, pl.ds(k * KW, KW)] = total.astype(BF)

    for r in range(REACH):
        for c in order:
            for side in range(2):
                copies(side, r, c).wait_send()


def per_device(*args):
    args = list(args)
    args[5] = args[5].T
    hbm = pl.BlockSpec(memory_space=pl.ANY)
    vmem = pl.BlockSpec(memory_space=pltpu.VMEM)
    smem = pl.BlockSpec(memory_space=pltpu.SMEM)
    return pl.pallas_call(
        kernel,
        out_shape=jax.ShapeDtypeStruct((1, 2, LAT, QH * RD), BF),
        in_specs=[hbm, smem, smem, vmem, vmem, hbm, hbm, vmem, hbm, hbm, hbm],
        out_specs=vmem,
        scratch_shapes=[
            pltpu.VMEM((ROWS, D), BF),
            pltpu.VMEM((3 * HA * HS, D), BF),
            pltpu.VMEM((HA * HS, D), BF),
            pltpu.VMEM((D, 2 * KW), BF),
            pltpu.VMEM((ROWS, D), BF),
            pltpu.VMEM((ROWS, 1792), BF),
            pltpu.VMEM((ROWS, 640), BF),
            pltpu.VMEM((ROWS, 640), BF),
            pltpu.VMEM((ROWS, D), BF),
            pltpu.VMEM((ROWS, 2 * KW), BF),
            pltpu.VMEM((16, 128), BF),
            pltpu.VMEM((KVH, 4 * LAT, 256), BF),
            pltpu.VMEM((LAT, QH * RD), BF),
            pltpu.VMEM((LAT, 2 * KW), BF),
            pltpu.VMEM((2, KVH, LAT, KW), BF),
            pltpu.VMEM((2, LAT, 128), F32),
            pltpu.VMEM((2, REACH, KVH, LAT, KW), BF),
            pltpu.VMEM((2, REACH, LAT, 128), F32),
            pltpu.VMEM((KVH, LAT, KW), F32),
            pltpu.VMEM((LAT, 128), F32),
            pltpu.SemaphoreType.DMA((16,)),
            pltpu.SemaphoreType.DMA((2, REACH, KVH + 1)),
            pltpu.SemaphoreType.DMA((2, REACH, KVH + 1)),
        ],
        compiler_params=pltpu.CompilerParams(
            collective_id=0, has_side_effects=True, vmem_limit_bytes=60 * 2**20
        ),
        cost_estimate=pl.CostEstimate(flops=4_300_000_000, bytes_accessed=9_000_000, transcendentals=1_600_000),
        name="tower_resampler",
    )(*args)


def solution(mesh):
    return jax.shard_map(
        per_device,
        mesh=mesh,
        in_specs=(
            P(("dp", "bal"), None, None),
            P("dp"),
            P("dp"),
            P(),
            P(),
            P(),
            P(),
            P(),
            P(),
            P(),
            P(),
        ),
        out_specs=P(("dp", "bal"), None, None, None),
        check_vma=False,
    )
```

profile of v0, /device:TPU:2, one launch (start us, length us, event | category | flops | bytes accessed | tf_op | source)
XLA Modules:
  0.0 57.2 jit_solution(9906366272398609787)
XLA Ops:
  0.0 55.4 %tower_resampler.1 = bf16[1,2,64,1536]{3,2,1,0:T(8,128)(2,1)} custom-call(bf16[2,256,1152]{2,1,0:T(8,128)(2,1)} %patches.1, s32[16]{0:T(128)} %counts.1, s32[16]{0:T(128)} %picks.1, f32[1152]{0:T(1024)} %ln_gain.1, f32[1152]{0:T(1024)} %ln_bias.1, bf16[1728,1152]{1,0:T(8,128)(2,1)} %bitcast.1, bf16[576,1152]{1,0:T(8,128)(2,1)} %w_out.1, f32[1152]{0:T(1024)} %ctx_gain.1, ...), custom_call_target="tpu_custom_call" | custom-call | flops 4300000256 | bytes 9000000 | tf_op jit(solution)/shard_map/tower_resampler/pallas_call | solution.py:382
  55.4 1.8 %copy.13 = bf16[1,2,64,1536]{3,2,1,0:T(8,128)(2,1)} copy(bf16[1,2,64,1536]{3,2,1,0:T(8,128)(2,1)} %tower_resampler.1) | data formatting | bytes 786432
where the time goes:
time: 57.3 us; the launch traced here: 57.2 us
  Pallas kernels  55.4 us (97%)
  local copies, waits for them, and re-layouts  1.77 us (3%)
    pallas_call x1, Pallas kernels, per_device(): pl.pallas_call(kernel, out_shape=jax.ShapeDtypeStruct((1, 2, LAT, QH * RD...  55.4 us
    unnamed x1, local copies, waits for them, and re-layouts  1.77 us

commit v1 on v0

v1 whole, which is shorter than its diff:
```python
import functools
import math

import jax
import jax.numpy as jnp
from jax import lax
from jax.experimental import pallas as pl
from jax.experimental.pallas import tpu as pltpu
from jax.sharding import PartitionSpec as P

D = 1152
HA = 8
HS = 72
PATCHES = 256
QH = 16
KVH = 4
RD = 96
LAT = 64
T = 2
IMAGES = 16
REACH = 4
ROWS = T * PATCHES
KW = KVH * RD
WA = HA * HS
EPS = 1e-6
NEG = -1e30
LOG2E = math.log2(math.e)
C_TOWER = LOG2E / math.sqrt(HS)
C_RES = LOG2E / math.sqrt(RD)
MESH = pl.DeviceIdType.MESH
F32 = jnp.float32
BF = jnp.bfloat16
NT = (((1,), (1,)), ((), ()))
KWIN = ((0, 128), (0, 256), (128, 256), (256, 128))
STAT = 96


def lanes(shape):
    return lax.broadcasted_iota(jnp.int32, shape, len(shape) - 1)


def dot(a, b):
    return jnp.dot(a, b, preferred_element_type=F32)


def dot_nt(a, b):
    return lax.dot_general(a, b, NT, preferred_element_type=F32)


def roll(x, shift):
    shift = shift % x.shape[-1]
    return x if shift == 0 else pltpu.roll(x, shift, 1)


def kernel(
    patches,
    counts_hbm,
    picks_hbm,
    ln_gain_hbm,
    ln_bias_hbm,
    w_qkv,
    w_out,
    ctx_gain_hbm,
    w_kv,
    latent_q,
    latent_kv,
    out,
    counts,
    picks,
    ln_gain,
    ln_bias,
    ctx_gain,
    xb,
    wq,
    wo,
    wk,
    nb,
    qv,
    kt,
    mix,
    fg,
    cx,
    qx,
    lq,
    lkv,
    send_o,
    send_s,
    got_o,
    got_s,
    lat_o,
    acc_r,
    acc_l,
    acc_1,
    ob,
    load_sem,
    send_sem,
    recv_sem,
    stat_send_sem,
    stat_recv_sem,
    out_sem,
    group_sem,
    factor,
    tops,
    sums,
    wt,
    last_r,
    last_l,
):
    me = lax.axis_index("bal")
    dp = lax.axis_index("dp")
    n = lax.axis_size("bal")

    loads = []

    def load(src, dst):
        copy = pltpu.make_async_copy(src, dst, load_sem.at[len(loads)])
        copy.start()
        loads.append(copy)
        return copy

    def wait(c):
        c.wait()

    x_loads = [load(patches.at[0], xb.at[pl.ds(0, PATCHES)])]
    small = [load(ln_gain_hbm, ln_gain), load(ln_bias_hbm, ln_bias)]
    x_loads.append(load(patches.at[1], xb.at[pl.ds(PATCHES, PATCHES)]))

    def group(g):
        row = pl.multiple_of(256 * g + jnp.where(g >= 2, 704, 0), 64)
        rows = pl.ds(row, 256)
        return pltpu.make_async_copy(w_qkv.at[rows], wq.at[rows], group_sem.at[g])

    for g in range(2):
        group(g).start()
    end_loads = [load(w_qkv.at[pl.ds(a, 64)], wq.at[pl.ds(a, 64)]) for a in (512, 2 * WA)]
    for g in range(2, 4):
        group(g).start()
    k_load = load(w_qkv.at[pl.ds(WA, WA)], wq.at[pl.ds(WA, WA)])
    wo_load = load(w_out, wo.at[pl.ds(64, WA)])
    small += [load(ctx_gain_hbm, ctx_gain), load(counts_hbm, counts), load(picks_hbm, picks)]
    lq_load = load(latent_q, lq)
    lkv_load = load(latent_kv, lkv)
    wk_load = load(w_kv, wk)

    got_o[...] = jnp.zeros_like(got_o)
    got_s[...] = jnp.zeros_like(got_s)
    tops[...] = jnp.zeros_like(tops)
    sums[...] = jnp.zeros_like(sums)
    wo[pl.ds(0, 64), :] = jnp.zeros((64, D), BF)
    kt[pl.ds(WA, 64), :] = jnp.zeros((64, ROWS), BF)

    def exists(side, distance):
        return me + distance < n if side == 0 else me - distance >= 0

    def at(side, distance):
        return (dp, me + distance if side == 0 else me - distance)

    barrier = pltpu.get_barrier_semaphore()
    for side in range(2):
        for distance in range(1, REACH + 1):

            @pl.when(exists(side, distance))
            def _(side=side, distance=distance):
                pl.semaphore_signal(barrier, inc=1, device_id=at(side, distance), device_id_type=MESH)

    def greeted():
        pl.semaphore_wait(barrier, jnp.minimum(me, REACH) + jnp.minimum(n - 1 - me, REACH))

    wait(small[0])
    wait(small[1])
    gain = ln_gain[...].reshape(1, D)
    bias = ln_bias[...].reshape(1, D)
    for c in x_loads:
        wait(c)

    def norm(i, _):
        rows = pl.ds(pl.multiple_of(i * 32, 32), 32)
        x = xb[rows, :].astype(F32)
        mean = jnp.mean(x, axis=-1, keepdims=True)
        c = x - mean
        var = jnp.mean(c * c, axis=-1, keepdims=True)
        nb[rows, :] = (c * lax.rsqrt(var + EPS) * gain + bias).astype(BF)
        return 0

    lax.fori_loop(0, ROWS // 32, norm, 0, unroll=4)

    def project(g, _):
        group(g).wait()
        rows = pl.ds(pl.multiple_of(256 * g + jnp.where(g >= 2, 704, 0), 64), 256)
        columns = pl.ds(pl.multiple_of(256 * g + jnp.where(g >= 2, 128, 0), 128), 256)
        qv[:, columns] = dot_nt(nb[...], wq[rows, :]).astype(BF)
        return 0

    lax.fori_loop(0, 4, project, 0)
    for c in end_loads:
        wait(c)
    ends_w = jnp.concatenate([wq[pl.ds(512, 64), :], wq[pl.ds(2 * WA, 64), :]], axis=0)
    qv[:, pl.ds(512, 128)] = dot_nt(nb[...], ends_w).astype(BF)
    wait(k_load)

    def project_keys(t, _):
        rows = pl.ds(pl.multiple_of(t * PATCHES, PATCHES), PATCHES)
        kt[pl.ds(0, WA), rows] = dot_nt(wq[pl.ds(WA, WA), :], nb[rows, :]).astype(BF)
        return 0

    lax.fori_loop(0, T, project_keys, 0)

    def tower(t, _):
        rows = pl.ds(pl.multiple_of(t * PATCHES, PATCHES), PATCHES)
        ln = lanes((PATCHES, 256))
        before = jnp.zeros((PATCHES, 128), F32)
        for i in range(HA // 2):
            q = qv[rows, pl.ds(128 * i, 256)]
            k = kt[pl.ds(128 * i, 256), rows]
            v = qv[rows, pl.ds(512 + 128 * i, 256)]
            mixed = jnp.zeros((PATCHES, 256), F32)
            for h in range(2):
                lo = 16 * i + HS * h
                mine = jnp.logical_and(ln >= lo, ln < lo + HS)
                s = dot(jnp.where(mine, q, jnp.zeros_like(q)), k)
                top = jnp.max(s, axis=-1, keepdims=True)
                e = jnp.exp2((s - top) * C_TOWER)
                total = jnp.sum(e, axis=-1, keepdims=True)
                o = dot(e.astype(BF), v) * (1.0 / total)
                lo += 64
                mixed = jnp.where(jnp.logical_and(ln >= lo, ln < lo + HS), o, mixed)
            mix[rows, pl.ds(128 * i, 128)] = (before + mixed[:, :128]).astype(BF)
            before = mixed[:, 128:]
        mix[rows, pl.ds(512, 128)] = before.astype(BF)
        return 0

    lax.fori_loop(0, T, tower, 0)

    wait(wo_load)
    wait(small[2])
    gain_c = ctx_gain[...].reshape(1, D)
    square = jnp.zeros((ROWS, 128), F32)
    for a in range(0, D, 256):
        w = min(256, D - a)
        f = dot(mix[...], wo[:, pl.ds(a, w)]) + xb[:, pl.ds(a, w)].astype(F32)
        f = f.astype(BF).astype(F32)
        for b in range(0, w, 128):
            square = square + f[:, b : b + 128] * f[:, b : b + 128]
        fg[:, pl.ds(a, w)] = (f * gain_c[:, a : a + w]).astype(BF)
    factor[...] = jnp.broadcast_to(
        lax.rsqrt(jnp.sum(square, axis=-1, keepdims=True) * (1.0 / D) + EPS), (ROWS, 128)
    )

    wait(wk_load)

    for a in range(0, 2 * KW, 256):
        c = dot(fg[...], wk[:, pl.ds(a, 256)])
        for b in (0, 128):
            cx[:, pl.ds(a + b, 128)] = (c[:, b : b + 128] * factor[...]).astype(BF)

    wait(lq_load)
    wait(lkv_load)
    ln = lanes((LAT, 128))
    for k in range(KVH):
        qt = [lq[:, pl.ds(k * KW + 128 * j, 128)].astype(F32) for j in range(3)]
        first, width = KWIN[k]
        for g in range(4):
            parts = []
            for b in range(first, first + width, 128):
                move = b - RD * k + RD * g
                acc = jnp.zeros((LAT, 128), F32)
                for j in range(3):
                    lo = max(RD * k - b, 0, 128 * j - move)
                    hi = min(RD * k + RD - b, 128, 128 * j + 128 - move)
                    if hi > lo:
                        moved = roll(qt[j], 128 * j - move)
                        acc = jnp.where(jnp.logical_and(ln >= lo, ln < hi), moved, acc)
                parts.append(acc)
            qx[k, pl.ds(g * LAT, LAT), pl.ds(0, width)] = jnp.concatenate(parts, axis=1).astype(BF)

    wait(small[3])
    wait(small[4])
    ends = []
    run = jnp.int32(0)
    for i in range(IMAGES):
        run = run + counts[i]
        ends.append(run)

    def image_of(tile):
        found = jnp.int32(0)
        for i in range(IMAGES):
            found = found + jnp.where(ends[i] <= tile, 1, 0)
        return found

    def flag(cond):
        return jnp.where(cond, F32(1.0), F32(0.0))

    def block(cond):
        return jnp.where(cond, F32(0.0), F32(NEG))

    firsts = [image_of(2 * (me + d)) for d in range(0, REACH + 1)]
    lasts = [jnp.where(me - d < 0, -1, image_of(2 * (me - d) + 1)) for d in range(0, REACH + 1)]
    img0, img1 = firsts[0], lasts[0]
    same = img0 == img1
    samef = flag(same)

    def owner_of(image):
        begin, end, pick = jnp.int32(0), jnp.int32(0), jnp.int32(0)
        for i in range(IMAGES):
            hit = image == i
            begin = jnp.where(hit, ends[i] - counts[i], begin)
            end = jnp.where(hit, ends[i], end)
            pick = jnp.where(hit, picks[i], pick)
        first, last = begin // 2, (end - 1) // 2
        return first + lax.rem(pick, last - first + 1)

    has0 = flag(owner_of(img0) == me)
    has1 = flag(jnp.logical_and(owner_of(img1) == me, jnp.logical_not(same)))

    def values(ref, rows, count, k):
        ln = lanes((count, 128))
        a, shift = RD * k // 128, -(RD * k % 128)
        one = roll(ref[rows, pl.ds(KW + 128 * a, 128)].astype(F32), shift)
        if RD * k + RD > 128 * (a + 1):
            two = roll(ref[rows, pl.ds(KW + 128 * (a + 1), 128)].astype(F32), shift)
            one = jnp.where(ln < 128 + shift, one, two)
        return jnp.where(ln < RD, one, 1.0).astype(BF)

    def scores(ref, rows, k):
        first, width = KWIN[k]
        s = dot_nt(qx[k, :, pl.ds(0, width)], ref[rows, pl.ds(first, width)])
        return s, jnp.max(s, axis=-1, keepdims=True)

    def weigh(ref, rows, count, k, s, top):
        e = jnp.exp2((s - top) * C_RES)
        return dot(e.astype(BF), values(ref, rows, count, k))

    def merge(parts):
        return jnp.concatenate(
            [
                jnp.where(ln < 96, parts[0], parts[1]),
                jnp.where(ln < 64, parts[1], parts[2]),
                jnp.where(ln < 32, parts[2], parts[3]),
            ],
            axis=1,
        )

    def dense(o):
        return merge([roll(o[LAT * g : LAT * g + LAT], RD * g) for g in range(4)])

    def compact(table, o, k):
        new = table[...]
        for g in range(4):
            part = jnp.broadcast_to(o[LAT * g : LAT * g + LAT], (LAT, 128))
            new = jnp.where(ln == STAT + 4 * k + g, part, new)
        table[...] = new

    def data(side, r, c):
        return pltpu.make_async_remote_copy(
            src_ref=send_o.at[side, c] if r == 0 else got_o.at[side, r - 1, c],
            dst_ref=got_o.at[side, r, c],
            send_sem=send_sem.at[side, r, c],
            recv_sem=recv_sem.at[side, r, c],
            device_id=at(side, 1),
            device_id_type=MESH,
        )

    def sends(side, r):
        return jnp.logical_and(exists(side, 1), exists(1 - side, r))

    def receives(side, r):
        return exists(1 - side, r + 1)

    def stats(side, r):
        slot = side * REACH + r
        return pltpu.make_async_remote_copy(
            src_ref=send_s.at[side],
            dst_ref=got_s.at[pl.ds(16 * slot, 16)],
            send_sem=stat_send_sem.at[side, r],
            recv_sem=stat_recv_sem.at[side, r],
            device_id=at(side, r + 1),
            device_id_type=MESH,
        )

    greeted()
    t0, t1 = pl.ds(0, PATCHES), pl.ds(PATCHES, PATCHES)

    def head(k):

        s0, top0 = scores(cx, t0, k)
        s1, top1 = scores(cx, t1, k)
        both = jnp.maximum(top0, top1)
        top0 = jnp.where(same, both, top0)
        top1 = jnp.where(same, both, top1)
        a0 = weigh(cx, t0, PATCHES, k, s0, top0)
        a1 = weigh(cx, t1, PATCHES, k, s1, top1)
        for side, (top, a) in enumerate(((top1, a1 + samef * a0), (top0, a0 + samef * a1))):
            send_o[side, k] = dense(a).astype(BF)

            @pl.when(sends(side, 0))
            def _(side=side):
                data(side, 0, k).start()

            compact(tops.at[side], top, k)
            compact(sums.at[side], a, k)

        sl, topl = scores(lkv, pl.ds(0, LAT), k)
        al = weigh(lkv, pl.ds(0, LAT), LAT, k, sl, topl)
        compact(tops.at[2], topl, k)
        compact(sums.at[2], al, k)
        lat_o[k] = dense(al)

    for k in range(KVH):
        head(k)

    for side in range(2):
        both = jnp.concatenate([tops[side] * C_RES, sums[side]], axis=0)
        send_s[side] = both.T[STAT : STAT + QH]
        for r in range(REACH):

            @pl.when(exists(side, r + 1))
            def _(side=side, r=r):
                stats(side, r).start()

    def arrive(side, r, c):
        @pl.when(receives(side, r))
        def _():
            data(side, r, c).wait_recv()

        if r + 1 < REACH:

            @pl.when(sends(side, r + 1))
            def _():
                data(side, r + 1, c).start()

    def forward(r):
        for side in range(2):

            def step(c, _, side=side):
                arrive(side, r, c)
                return 0

            lax.fori_loop(0, KVH, step, 0)

    forward(0)
    forward(1)

    for side in range(2):
        for r in range(REACH):

            @pl.when(exists(1 - side, r + 1))
            def _(side=side, r=r):
                stats(side, r).wait_recv()

    table = got_s[...].T
    all_tops, all_sums = table[:LAT], table[LAT:]

    def of_source(x, slot):
        return roll(x, STAT - 16 * slot)

    own = [(tops[side] * C_RES, sums[side]) for side in range(2)]
    latent = (tops[2] * C_RES, sums[2])
    r_src = [
        (of_source(all_tops, r) + block(lasts[r + 1] == img0), of_source(all_sums, r)) for r in range(REACH)
    ]
    l_src = [
        (of_source(all_tops, REACH + r) + block(firsts[r + 1] == img1), of_source(all_sums, REACH + r))
        for r in range(REACH)
    ]
    apart = block(jnp.logical_not(same))
    together = block(same)
    slots = (
        [own[1], latent] + r_src + [(t + together, s) for t, s in l_src],
        [own[0], latent] + [(t + apart, s) for t, s in l_src],
    )
    weights = []
    for slot in slots:
        top = functools.reduce(jnp.maximum, [t for t, _ in slot])
        es = [jnp.exp2(t - top) for t, _ in slot]
        inv = 1.0 / functools.reduce(jnp.add, [e * s for e, (_, s) in zip(es, slot)])
        weights.append([e * inv for e in es])
    w_own0, w_lat0 = weights[0][:2]
    w_own1, w_lat1 = weights[1][:2]
    w_r = weights[0][2 : 2 + REACH]
    w_l = [a + b for a, b in zip(weights[0][2 + REACH :], weights[1][2:])]

    for i, w in enumerate([w_own0, w_lat0, w_own1, w_lat1] + w_r + w_l):
        wt[i] = w

    def spread(i, k):
        w = pltpu.roll(wt[i], lax.rem(128 - 4 * k, 128), 1)
        return merge([jnp.broadcast_to(w[:, STAT + g : STAT + g + 1], (LAT, 128)) for g in range(4)])

    def start(k, _):
        lat = lat_o[k]
        acc_r[k] = spread(0, k) * send_o[1, k].astype(F32) + spread(1, k) * lat
        acc_1[k] = spread(2, k) * send_o[0, k].astype(F32) + spread(3, k) * lat
        acc_l[k] = jnp.zeros((LAT, KW), F32)
        return 0

    lax.fori_loop(0, KVH, start, 0)

    def absorb(r):
        def step(k, _):
            acc_r[k] += spread(4 + r, k) * got_o[0, r, k].astype(F32)
            acc_l[k] += spread(8 + r, k) * got_o[1, r, k].astype(F32)
            return 0

        lax.fori_loop(0, KVH, step, 0)

    forward(2)
    for r in range(REACH - 1):
        absorb(r)

    def last_weights(k, _):
        last_r[k] = spread(4 + REACH - 1, k)
        last_l[k] = spread(8 + REACH - 1, k)
        return 0

    lax.fori_loop(0, KVH, last_weights, 0)

    def result(k):
        return pltpu.make_async_copy(ob.at[k], out.at[0, :, :, pl.ds(pl.multiple_of(k * KW, 128), KW)], out_sem.at[k])

    def finish_r(k, _):
        arrive(0, REACH - 1, k)
        acc_r[k] += last_r[k] * got_o[0, REACH - 1, k].astype(F32)
        return 0

    def finish_l(k, _):
        arrive(1, REACH - 1, k)
        from_l = acc_l[k] + last_l[k] * got_o[1, REACH - 1, k].astype(F32)
        ob[k, 0] = ((acc_r[k] + samef * from_l) * has0).astype(BF)
        ob[k, 1] = ((acc_1[k] + (1.0 - samef) * from_l) * has1).astype(BF)
        result(k).start()
        return 0

    lax.fori_loop(0, KVH, finish_r, 0)
    lax.fori_loop(0, KVH, finish_l, 0)

    for side in range(2):
        for r in range(REACH):

            @pl.when(exists(side, r + 1))
            def _(side=side, r=r):
                stats(side, r).wait_send()

            for c in range(KVH):

                @pl.when(sends(side, r))
                def _(side=side, r=r, c=c):
                    data(side, r, c).wait_send()

    for k in range(KVH):
        result(k).wait()


def per_device(*args):
    args = list(args)
    args[5] = args[5].T
    hbm = pl.BlockSpec(memory_space=pl.ANY)
    vmem, smem, dma = pltpu.VMEM, pltpu.SMEM, pltpu.SemaphoreType.DMA
    return pl.pallas_call(
        kernel,
        out_shape=jax.ShapeDtypeStruct((1, 2, LAT, QH * RD), BF),
        in_specs=[hbm] * 11,
        out_specs=hbm,
        scratch_shapes=[
            smem((IMAGES,), jnp.int32),
            smem((IMAGES,), jnp.int32),
            vmem((D,), F32),
            vmem((D,), F32),
            vmem((D,), F32),
            vmem((ROWS, D), BF),
            vmem((3 * WA, D), BF),
            vmem((640, D), BF),
            vmem((D, 2 * KW), BF),
            vmem((ROWS, D), BF),
            vmem((ROWS, D), BF),
            vmem((640, ROWS), BF),
            vmem((ROWS, 640), BF),
            vmem((ROWS, D), BF),
            vmem((ROWS, 2 * KW), BF),
            vmem((KVH, 4 * LAT, 256), BF),
            vmem((LAT, QH * RD), BF),
            vmem((LAT, 2 * KW), BF),
            vmem((2, KVH, LAT, KW), BF),
            vmem((2, QH, 128), F32),
            vmem((2, REACH, KVH, LAT, KW), BF),
            vmem((2 * REACH * 16, 128), F32),
            vmem((KVH, LAT, KW), F32),
            vmem((KVH, LAT, KW), F32),
            vmem((KVH, LAT, KW), F32),
            vmem((KVH, LAT, KW), F32),
            vmem((KVH, 2, LAT, KW), BF),
            dma((24,)),
            dma((2, REACH, KVH)),
            dma((2, REACH, KVH)),
            dma((2, REACH)),
            dma((2, REACH)),
            dma((KVH,)),
            dma((4,)),
            vmem((ROWS, 128), F32),
            vmem((3, LAT, 128), F32),
            vmem((3, LAT, 128), F32),
            vmem((12, LAT, 128), F32),
            vmem((KVH, LAT, KW), F32),
            vmem((KVH, LAT, KW), F32),
        ],
        compiler_params=pltpu.CompilerParams(
            collective_id=0, has_side_effects=True, vmem_limit_bytes=60 * 2**20
        ),
        cost_estimate=pl.CostEstimate(flops=4_300_000_000, bytes_accessed=9_000_000, transcendentals=1_600_000),
        name="tower_resampler",
    )(*args)


def solution(mesh):
    return jax.shard_map(
        per_device,
        mesh=mesh,
        in_specs=(
            P(("dp", "bal"), None, None),
            P("dp"),
            P("dp"),
            P(),
            P(),
            P(),
            P(),
            P(),
            P(),
            P(),
            P(),
        ),
        out_specs=P(("dp", "bal"), None, None, None),
        check_vma=False,
    )
```

time: 57.3 us -> 42.1 us (0.73)
  the two profiles are of different devices: /device:TPU:2 before, /device:TPU:28 now
where the time goes in v1:
time: 42.1 us; the launch traced here: 42 us
  Pallas kernels  40.2 us (95%)
  local copies, waits for them, and re-layouts  1.77 us (4%)
    pallas_call x1, Pallas kernels, per_device(): pl.pallas_call(kernel, out_shape=jax.ShapeDtypeStruct((1, 2, LAT, QH * RD...  40.2 us
    unnamed x1, local copies, waits for them, and re-layouts  1.77 us

profile of v1, /device:TPU:28, one launch (start us, length us, event | category | flops | bytes accessed | tf_op | source)
XLA Modules:
  0.0 42.0 jit_solution(6524832806641487982)
XLA Ops:
  0.0 40.2 %tower_resampler.1 = bf16[1,2,64,1536]{3,2,1,0:T(8,128)(2,1)} custom-call(bf16[2,256,1152]{2,1,0:T(8,128)(2,1)} %patches.1, s32[16]{0:T(128)} %counts_hbm.1, s32[16]{0:T(128)} %picks_hbm.1, f32[1152]{0:T(1024)} %ln_gain_hbm.1, f32[1152]{0:T(1024)} %ln_bias_hbm.1, bf16[1728,1152]{1,0:T(8,128)(2,1)} %bitcast.1, bf16[576,1152]{1,0:T(8,128)(2,1)} %w_out.1, ...), custom_call_target="tpu_custom_call" | custom-call | flops 4300000256 | bytes 9000000 | tf_op jit(solution)/shard_map/tower_resampler/pallas_call | solution.py:558
  40.3 1.8 %copy.13 = bf16[1,2,64,1536]{3,2,1,0:T(8,128)(2,1)} copy(bf16[1,2,64,1536]{3,2,1,0:T(8,128)(2,1)} %tower_resampler.1) | data formatting | bytes 786432

commit v2 on v1

--- a/solution.py
+++ b/solution.py
@@ -184,26 +184,24 @@
 
     lax.fori_loop(0, ROWS // 32, norm, 0, unroll=4)
 
-    def project(g, _):
+    for g in range(4):
         group(g).wait()
-        rows = pl.ds(pl.multiple_of(256 * g + jnp.where(g >= 2, 704, 0), 64), 256)
-        columns = pl.ds(pl.multiple_of(256 * g + jnp.where(g >= 2, 128, 0), 128), 256)
-        qv[:, columns] = dot_nt(nb[...], wq[rows, :]).astype(BF)
-        return 0
-
-    lax.fori_loop(0, 4, project, 0)
     for c in end_loads:
         wait(c)
-    ends_w = jnp.concatenate([wq[pl.ds(512, 64), :], wq[pl.ds(2 * WA, 64), :]], axis=0)
-    qv[:, pl.ds(512, 128)] = dot_nt(nb[...], ends_w).astype(BF)
     wait(k_load)
 
-    def project_keys(t, _):
+    def project(t, _):
         rows = pl.ds(pl.multiple_of(t * PATCHES, PATCHES), PATCHES)
-        kt[pl.ds(0, WA), rows] = dot_nt(wq[pl.ds(WA, WA), :], nb[rows, :]).astype(BF)
-        return 0
-
-    lax.fori_loop(0, T, project_keys, 0)
+        x = nb[rows, :]
+        for g in range(4):
+            a, c = 256 * g + (704 if g >= 2 else 0), 256 * g + (128 if g >= 2 else 0)
+            qv[rows, pl.ds(c, 256)] = dot_nt(x, wq[pl.ds(a, 256), :]).astype(BF)
+        ends_w = jnp.concatenate([wq[pl.ds(512, 64), :], wq[pl.ds(2 * WA, 64), :]], axis=0)
+        qv[rows, pl.ds(512, 128)] = dot_nt(x, ends_w).astype(BF)
+        kt[pl.ds(0, WA), rows] = dot_nt(wq[pl.ds(WA, WA), :], x).astype(BF)
+        return 0
+
+    lax.fori_loop(0, T, project, 0)
 
     def tower(t, _):
         rows = pl.ds(pl.multiple_of(t * PATCHES, PATCHES), PATCHES)
@@ -248,10 +246,16 @@
 
     wait(wk_load)
 
-    for a in range(0, 2 * KW, 256):
-        c = dot(fg[...], wk[:, pl.ds(a, 256)])
-        for b in (0, 128):
-            cx[:, pl.ds(a + b, 128)] = (c[:, b : b + 128] * factor[...]).astype(BF)
+
+    def context(t, _):
+        rows = pl.ds(pl.multiple_of(t * PATCHES, PATCHES), PATCHES)
+        for a in range(0, 2 * KW, 256):
+            c = dot(fg[rows, :], wk[:, pl.ds(a, 256)])
+            for b in (0, 128):
+                cx[rows, pl.ds(a + b, 128)] = (c[:, b : b + 128] * factor[rows, :]).astype(BF)
+        return 0
+
+    lax.fori_loop(0, T, context, 0)
 
     wait(lq_load)
     wait(lkv_load)
@@ -399,6 +403,40 @@
             compact(tops.at[side], top, k)
             compact(sums.at[side], a, k)
 
+    for k in range(KVH):
+        head(k)
+
+    for side in range(2):
+        both = jnp.concatenate([tops[side] * C_RES, sums[side]], axis=0)
+        send_s[side] = both.T[STAT : STAT + QH]
+        for r in range(REACH):
+
+            @pl.when(exists(side, r + 1))
+            def _(side=side, r=r):
+                stats(side, r).start()
+
+    def arrive(side, r, c):
+        @pl.when(receives(side, r))
+        def _():
+            data(side, r, c).wait_recv()
+
+        if r + 1 < REACH:
+
+            @pl.when(sends(side, r + 1))
+            def _():
+                data(side, r + 1, c).start()
+
+    def forward(r):
+        def step(c, _):
+            for side in range(2):
+                arrive(side, r, c)
+            return 0
+
+        lax.fori_loop(0, KVH, step, 0)
+
+    forward(0)
+
+    def latent_head(k):
         sl, topl = scores(lkv, pl.ds(0, LAT), k)
         al = weigh(lkv, pl.ds(0, LAT), LAT, k, sl, topl)
         compact(tops.at[2], topl, k)
@@ -406,38 +444,8 @@
         lat_o[k] = dense(al)
 
     for k in range(KVH):
-        head(k)
-
-    for side in range(2):
-        both = jnp.concatenate([tops[side] * C_RES, sums[side]], axis=0)
-        send_s[side] = both.T[STAT : STAT + QH]
-        for r in range(REACH):
-
-            @pl.when(exists(side, r + 1))
-            def _(side=side, r=r):
-                stats(side, r).start()
-
-    def arrive(side, r, c):
-        @pl.when(receives(side, r))
-        def _():
-            data(side, r, c).wait_recv()
-
-        if r + 1 < REACH:
-
-            @pl.when(sends(side, r + 1))
-            def _():
-                data(side, r + 1, c).start()
-
-    def forward(r):
-        for side in range(2):
-
-            def step(c, _, side=side):
-                arrive(side, r, c)
-                return 0
-
-            lax.fori_loop(0, KVH, step, 0)
-
-    forward(0)
+        latent_head(k)
+
     forward(1)
 
     for side in range(2):

time: 42.1 us -> 40.3 us (0.957)
  Pallas kernels: 40.2 us -> 38.4 us
    pallas_call x1, Pallas kernels: 40.2 us -> 38.4 us  [per_device(): pl.pallas_call(kernel, out_shape=jax.ShapeDtypeStruct((1, 2, LAT, QH * RD...]
where the time goes in v2:
time: 40.3 us; the launch traced here: 40.2 us
  Pallas kernels  38.4 us (95%)
  local copies, waits for them, and re-layouts  1.77 us (4%)
    pallas_call x1, Pallas kernels, per_device(): pl.pallas_call(kernel, out_shape=jax.ShapeDtypeStruct((1, 2, LAT, QH * RD...  38.4 us
    unnamed x1, local copies, waits for them, and re-layouts  1.77 us

profile of v2, /device:TPU:28, one launch (start us, length us, event | category | flops | bytes accessed | tf_op | source)
XLA Modules:
  0.0 40.2 jit_solution(3205939326175479777)
XLA Ops:
  0.0 38.4 %tower_resampler.1 = bf16[1,2,64,1536]{3,2,1,0:T(8,128)(2,1)} custom-call(bf16[2,256,1152]{2,1,0:T(8,128)(2,1)} %patches.1, s32[16]{0:T(128)} %counts_hbm.1, s32[16]{0:T(128)} %picks_hbm.1, f32[1152]{0:T(1024)} %ln_gain_hbm.1, f32[1152]{0:T(1024)} %ln_bias_hbm.1, bf16[1728,1152]{1,0:T(8,128)(2,1)} %bitcast.1, bf16[576,1152]{1,0:T(8,128)(2,1)} %w_out.1, ...), custom_call_target="tpu_custom_call" | custom-call | flops 4300000256 | bytes 9000000 | tf_op jit(solution)/shard_map/tower_resampler/pallas_call | solution.py:566
  38.4 1.8 %copy.13 = bf16[1,2,64,1536]{3,2,1,0:T(8,128)(2,1)} copy(bf16[1,2,64,1536]{3,2,1,0:T(8,128)(2,1)} %tower_resampler.1) | data formatting | bytes 786432
